TPU v7x, 32 devices: a whole 2x2x4 slice. The times are simulated.
32 devices in a mesh: row: 16 (over z, x, core), col: 2 (over y).
Axes of the slice: x: 2, y: 2, z: 4, core: 2. Of those that a mesh axis runs over, the one named last changes fastest.
Arguments:
- object_field: float32 [2, 2, 2048, 256], P(None, None, 'row', 'col'), may hold values from -1 to 1
- probe: float32 [4, 2, 128, 128], replicated, may hold values from -3 to 3
- kernel_phase: float32 [128, 128], replicated, may hold values from -3.140625 to 3.140625
- amplitudes: float32 [3, 16, 2, 128, 128], P(None, 'row', 'col'), may hold values from 0.05 to 1
- offsets: int32 [3, 16, 2, 2], P(None, 'row', 'col'), may hold values from 0 to 64
Outputs:
- object_out: float32 [2, 2, 2048, 256], P(None, None, 'row', 'col')
- probe_out: float32 [4, 2, 128, 128], replicated
Inputs may be any that keep to these rules, and one draw needn't show every extreme that they name: offsets[b, r + p, c] place a window of 128 x 128 pixels inside tile (r, c) extended by 32 pixels on each side.
All inputs are finite; a program needn't handle non-finite values.
Results may differ from a plain program's by a relative error of at most 0.0003.
Values sent between devices are 32-bit elements; how exact they have to be, the bound alone decides.
A program may use at most 128 MiB of HBM per device.

v0:
```python
import functools
import math

import jax
import jax.numpy as jnp
import numpy as np
from jax import lax
from jax.experimental import pallas as pl
from jax.experimental.pallas import tpu as pltpu
from jax.sharding import PartitionSpec as P

OVL = 32
OBJECT_RATE = 0.5
PROBE_RATE = 0.5
FLOOR = 0.1
MESH = pl.DeviceIdType.MESH
F32 = jnp.float32
BF16 = jnp.bfloat16

SIDES = ((-1, 0), (1, 0), (0, -1), (0, 1), (-1, -1), (-1, 1), (1, -1), (1, 1))


def split(values):
    high = values.astype(BF16)
    return high, (values - high.astype(F32)).astype(BF16)


def dft_matrices(window):
    counter = np.arange(window)
    phases = (counter[:, None] * counter[None, :] % window) * (-2.0 * np.pi / window)
    c, s = np.cos(phases) / math.sqrt(window), np.sin(phases) / math.sqrt(window)
    left = np.block([[c, -s], [s, c]]).astype(np.float32)
    out = []
    for m in (left, left.T):
        high = m.astype(BF16)
        out += [high, (m - high.astype(np.float32)).astype(BF16)]
    return np.stack(out)


def dot(a, b):
    return jnp.dot(a, b, preferred_element_type=F32)


def product(a, b):
    return dot(a[0], b[0]) + (dot(a[0], b[1]) + dot(a[1], b[0]))


def dft(fields, tables, inverse):
    first, second = (tables[1], tables[0]) if inverse else tables
    w = fields[0][0].shape[0]
    x = jnp.concatenate(
        [jnp.concatenate([f[k] for f in fields], axis=1) for k in range(2)], axis=0
    )
    y = product(first, split(x))
    z = jnp.concatenate(
        [
            jnp.concatenate([y[:w, m * w : m * w + w], y[w:, m * w : m * w + w]], axis=1)
            for m in range(len(fields))
        ],
        axis=0,
    )
    r = product(split(z), second)
    return [(r[m * w : m * w + w, :w], r[m * w : m * w + w, w:]) for m in range(len(fields))]


def cmul(a, b):
    return a[0] * b[0] - a[1] * b[1], a[0] * b[1] + a[1] * b[0]


def conj_mul(a, b):
    return a[0] * b[0] + a[1] * b[1], a[0] * b[1] - a[1] * b[0]


def csum(pairs):
    re, im = pairs[0]
    for p in pairs[1:]:
        re, im = re + p[0], im + p[1]
    return re, im


def stages_of(rows, n_row, n_col):
    out = []
    for group, n in (("core", 2), ("col", n_col), ("rest", n_row // 2)):
        if n < 2:
            continue
        scatter = rows % (8 * n) == 0
        rows = rows // n if scatter else rows
        out.append((group, n, scatter, rows))
    return out


def kernel(
    n_row, n_col, batches, modes, stages,
    off_ref, obj_ref, probe_ref, phase_ref, amp_ref, tab_ref,
    obj_out, probe_out,
    ext, ziel, grad, strip, from_row, from_col, from_corner,
    phi_ref, kern_ref, pnow, acc, gat, *rest,
):
    stage_bufs = rest[: len(stages)]
    ex_send, ex_recv, rs_send, rs_recv, ag_send, ag_recv = rest[len(stages) :]
    w = obj_ref.shape[-1]
    full = w + 2 * OVL
    band = 2 * OVL
    row, col = lax.axis_index("row"), lax.axis_index("col")

    def there(dr, dc):
        ok = None
        if dr:
            ok = row > 0 if dr < 0 else row < n_row - 1
        if dc:
            c = col > 0 if dc < 0 else col < n_col - 1
            ok = c if ok is None else jnp.logical_and(ok, c)
        return ok

    def member(group, d):
        if group == "core":
            return row + 1 - 2 * lax.rem(row, 2), col
        if group == "col":
            return row, lax.rem(col + d, n_col)
        n = n_row // 2
        return 2 * lax.rem(lax.div(row, 2) + d, n) + lax.rem(row, 2), col

    def rank(group):
        if group == "core":
            return lax.rem(row, 2)
        return col if group == "col" else lax.div(row, 2)

    barrier = pltpu.get_barrier_semaphore()
    expected = 0
    for dr, dc in SIDES:
        ok = there(dr, dc)
        expected = expected + ok.astype(jnp.int32)

        @pl.when(ok)
        def _():
            pl.semaphore_signal(
                barrier, inc=1, device_id=(row + dr, col + dc), device_id_type=MESH
            )

    for group, n, _, _ in stages:
        for d in range(1, n):
            pl.semaphore_signal(barrier, inc=1, device_id=member(group, d), device_id_type=MESH)
        expected = expected + (n - 1)

    lane = lax.broadcasted_iota(jnp.int32, (full, w), 1)
    line = lax.broadcasted_iota(jnp.int32, (full, w), 0)
    low, high = lane < OVL, lane >= w - OVL
    left_part = high | ((lane >= OVL) & (lane < 2 * OVL))
    top, bottom = row == 0, row == n_row - 1
    row_ok = (jnp.logical_not(top) | (line >= OVL)) & (jnp.logical_not(bottom) | (line < w + OVL))
    at_left, at_right = col == 0, col == n_col - 1
    col_ok = (left_part & jnp.logical_not(at_left)) | (
        jnp.logical_not(left_part) & jnp.logical_not(at_right)
    )
    side_ok = row_ok & col_ok

    def swap(x):
        return pltpu.roll(x, w // 2, x.ndim - 1)

    def send(e):
        for p in range(2):
            side, a, b = grad[e, 4 + p], grad[e, 2 * p], swap(grad[e, 2 * p + 1])
            strip[e, 0, p] = jnp.where(left_part, side, jnp.where(low, a, b))
            strip[e, 1, p] = jnp.where(left_part, jnp.where(high, a, b), side)
        for k in range(8):
            dr, dc = SIDES[k]

            @pl.when(there(dr, dc))
            def _():
                copy_of(e, k).start()

    def copy_of(e, k):
        dr, dc = SIDES[k]
        rows = pl.ds(0 if dr < 0 else w, band)
        if dc == 0:
            src, dst = grad.at[e, :, rows], from_row.at[e, k]
        elif dr == 0:
            src, dst = strip.at[e, k - 2], from_col.at[e, k - 2]
        else:
            src, dst = strip.at[e, 0 if dc < 0 else 1, :, rows], from_corner.at[e, k - 4]
        return pltpu.make_async_remote_copy(
            src_ref=src, dst_ref=dst, send_sem=ex_send.at[e, k], recv_sem=ex_recv.at[e, k],
            device_id=(row + dr, col + dc), device_id_type=MESH,
        )

    def receive(e, scale):
        for f in range(6):
            ext[f] = ext[f] + scale * grad[e, f] if e else grad[e, f]
        for k in range(8):
            dr, dc = SIDES[k]

            @pl.when(there(-dr, -dc))
            def _():
                copy_of(e, k).wait_recv()
                rows = pl.ds(w if dr < 0 else 0, band)
                if dc == 0:
                    for f in range(6):
                        ext[f, rows] = ext[f, rows] + scale * from_row[e, k, f]
                    return
                if dr == 0:
                    rows = pl.ds(0, full)
                count = full if dr == 0 else band
                lp, lo, hi = left_part[:count], low[:count], high[:count]
                for p in range(2):
                    x = from_col[e, k - 2, p] if dr == 0 else from_corner[e, k - 4, p]
                    x = scale * x
                    y = swap(x)
                    edge, mine = (lo, lp) if dc > 0 else (hi, jnp.logical_not(lp))
                    ext[4 + p, rows] = ext[4 + p, rows] + jnp.where(mine, x, 0.0)
                    ext[2 * p, rows] = ext[2 * p, rows] + jnp.where(edge, x, 0.0)
                    ext[2 * p + 1, rows] = ext[2 * p + 1, rows] + jnp.where(edge, y, 0.0)

    def sent(e):
        for k in range(8):
            dr, dc = SIDES[k]

            @pl.when(there(dr, dc))
            def _():
                copy_of(e, k).wait_send()

    def base_of(s):
        rows = acc.shape[1]
        base = 0
        for group, n, scatter, after in stages[:s]:
            if scatter:
                base = base + rank(group) * after
        return base

    def rs_copies(q, s):
        group, n, scatter, after = stages[s]
        base, mine = base_of(s), rank(group)
        for d in range(1, n):
            to = lax.rem(mine + d, n)
            start = pl.multiple_of(base + (to * after if scatter else 0), 8)
            slot = d - 1 if scatter else mine
            yield pltpu.make_async_remote_copy(
                src_ref=acc.at[q, pl.ds(start, after)], dst_ref=stage_bufs[s].at[q, slot],
                send_sem=rs_send.at[q, s, d], recv_sem=rs_recv.at[q, s, d],
                device_id=member(group, d), device_id_type=MESH,
            )

    def rs_start(q, s):
        for c in rs_copies(q, s):
            c.start()

    def rs_end(q, s):
        group, n, scatter, after = stages[s]
        start = pl.multiple_of(base_of(s + 1), 8)
        place = pl.ds(start, after)
        buf = stage_bufs[s]
        if not scatter:
            buf[q, rank(group)] = acc[q, place]
        for c in rs_copies(q, s):
            c.wait()
        total = acc[q, place] if scatter else buf[q, 0]
        for j in range(0 if scatter else 1, n - 1 if scatter else n):
            total = total + buf[q, j]
        if s == len(stages) - 1:
            gat[q, place] = total
        else:
            acc[q, place] = total

    def ag_copies(q, s):
        group, n, scatter, after = stages[s]
        place = pl.ds(pl.multiple_of(base_of(s + 1), 8), after)
        for d in range(1, n if scatter else 1):
            yield pltpu.make_async_remote_copy(
                src_ref=gat.at[q, place], dst_ref=gat.at[q, place],
                send_sem=ag_send.at[q, s, d], recv_sem=ag_recv.at[q, s, d],
                device_id=member(group, d), device_id_type=MESH,
            )

    def ag_start(q, s):
        for c in ag_copies(q, s):
            c.start()

    def ag_end(q, s):
        for c in ag_copies(q, s):
            c.wait()

    def sum_steps(q):
        steps = []
        last = len(stages) - 1
        for s in range(last + 1):
            steps.append((lambda s=s: rs_start(q, s), lambda s=s: rs_end(q, s)))
        for s in range(last, -1, -1):
            steps.append((lambda s=s: ag_start(q, s), lambda s=s: ag_end(q, s)))
        return steps

    running = []

    def advance():
        if running:
            running.pop(0)[1]()
            if running:
                running[0][0]()

    for f in range(6):
        grad[0, f] = jnp.zeros((full, w), F32)
    for f in range(4):
        grad[0, f, OVL : OVL + w] = obj_ref[f]
    pl.semaphore_wait(barrier, expected)
    send(0)
    kern_ref[0] = jnp.cos(phase_ref[...])
    kern_ref[1] = jnp.sin(phase_ref[...])
    ziel[...] = jnp.zeros_like(ziel)
    receive(0, 1.0)

    rate = PROBE_RATE / math.sqrt(n_row * n_col)
    kern = (kern_ref[0], kern_ref[1])
    conj_kern = (kern[0], -kern[1])
    tables = ((tab_ref[0], tab_ref[1]), (tab_ref[2], tab_ref[3]))
    lane_w = lax.broadcasted_iota(jnp.int32, (w, w), 1)

    for b in range(batches):
        if b == 0 or b == 1:
            source = probe_ref
        else:
            while running:
                advance()
            previous = probe_ref if b == 2 else pnow
            for m in range(modes):
                for k in range(2):
                    at = (m * 2 + k) * w
                    pnow[m, k] = previous[m, k] - rate * gat[b - 2, at : at + w]
            source = pnow
        y0, x0 = off_ref[b, 0], off_ref[b, 1]
        start = x0 - OVL
        back = lax.rem(w - start, w)
        back_half = lax.rem(w + w // 2 - start, w)
        inside = (lane_w + start >= 0) & (lane_w + start < w)

        def window(f):
            main = ext[f, pl.ds(y0, w), :]
            side = ext[4 + f // 2, pl.ds(y0, w), :]
            return jnp.where(
                inside,
                pltpu.roll(main, back, 1),
                pltpu.roll(side, back_half if f % 2 else back, 1),
            )

        o1, o2 = (window(0), window(1)), (window(2), window(3))
        probe = [(source[m, 0], source[m, 1]) for m in range(modes)]
        spectrum = dft([cmul(p, o1) for p in probe], tables, False)
        phi = dft([cmul(v, kern) for v in spectrum], tables, True)
        for m in range(modes):
            phi_ref[m, 0], phi_ref[m, 1] = phi[m]
        advance()
        far = dft([cmul(v, o2) for v in phi], tables, False)
        intensity = far[0][0] * far[0][0] + far[0][1] * far[0][1]
        for v in far[1:]:
            intensity = intensity + (v[0] * v[0] + v[1] * v[1])
        factor = 1.0 - amp_ref[b] / jnp.sqrt(intensity + FLOOR)
        chi2 = dft([(v[0] * factor, v[1] * factor) for v in far], tables, True)
        advance()
        g2 = csum([conj_mul((phi_ref[m, 0], phi_ref[m, 1]), chi2[m]) for m in range(modes)])
        spectrum = dft([conj_mul(o2, v) for v in chi2], tables, False)
        chi1 = dft([cmul(v, conj_kern) for v in spectrum], tables, True)
        advance()
        probe = [(source[m, 0], source[m, 1]) for m in range(modes)]
        g1 = csum([conj_mul(probe[m], chi1[m]) for m in range(modes)])
        for f, g in enumerate((*g1, *g2)):
            ziel[f, 2 * OVL : 2 * OVL + w] = g
        ahead = lax.rem(w + start, w)
        outside = (lane - start < 0) | (lane - start >= w)
        others = []
        for f in range(4):
            moved = pltpu.roll(ziel[f, pl.ds(2 * OVL - y0, full), :], ahead, 1)
            grad[b + 1, f] = jnp.where(row_ok & jnp.logical_not(outside), moved, 0.0)
            others.append(jnp.where(outside, moved, 0.0))
        for p in range(2):
            grad[b + 1, 4 + p] = jnp.where(
                side_ok, others[2 * p] + swap(others[2 * p + 1]), 0.0
            )
        send(b + 1)
        advance()
        q = min(b, max(batches - 2, 0))
        for m in range(modes):
            g = conj_mul(o1, chi1[m])
            for k in range(2):
                at = pl.ds((m * 2 + k) * w, w)
                acc[q, at] = g[k] if b == q else acc[q, at] + g[k]
        if b != batches - 2 or batches == 1:
            while running:
                advance()
            running.extend(sum_steps(q))
            running[0][0]()
        receive(b + 1, -OBJECT_RATE)
        if b < batches - 1:
            advance()
        if b == batches - 1:
            for f in range(4):
                obj_out[f] = ext[f, OVL : OVL + w]

    while running:
        advance()
    q = max(batches - 2, 0)
    last = pnow if batches > 2 else probe_ref
    for m in range(modes):
        for k in range(2):
            at = (m * 2 + k) * w
            probe_out[m, k] = last[m, k] - rate * gat[q, at : at + w]
    for e in range(batches + 1):
        sent(e)


def per_device(n_row, n_col, object_field, probe, kernel_phase, amplitudes, offsets):
    batches = amplitudes.shape[0]
    modes, _, w, _ = probe.shape
    full = w + 2 * OVL
    rows = modes * 2 * w
    stages = stages_of(rows, n_row, n_col)
    sums = max(batches - 1, 1)
    most = max(n for _, n, _, _ in stages)
    vmem, smem = pltpu.VMEM, pltpu.SMEM
    dma = pltpu.SemaphoreType.DMA
    scratch = [
        vmem((6, full, w), F32),
        vmem((4, full + 2 * OVL, w), F32),
        vmem((batches + 1, 6, full, w), F32),
        vmem((batches + 1, 2, 2, full, w), F32),
        vmem((batches + 1, 2, 6, 2 * OVL, w), F32),
        vmem((batches + 1, 2, 2, full, w), F32),
        vmem((batches + 1, 4, 2, 2 * OVL, w), F32),
        vmem((modes, 2, w, w), F32),
        vmem((2, w, w), F32),
        vmem((modes, 2, w, w), F32),
        vmem((sums, rows, w), F32),
        vmem((sums, rows, w), F32),
    ]
    for _, n, scatter, after in stages:
        scratch.append(vmem((sums, n - 1 if scatter else n, after, w), F32))
    scratch += [dma((batches + 1, 8))] * 2 + [dma((sums, len(stages), most))] * 4
    whole = pl.BlockSpec(memory_space=vmem)
    obj, new_probe = pl.pallas_call(
        functools.partial(kernel, n_row, n_col, batches, modes, stages),
        out_shape=(
            jax.ShapeDtypeStruct((4, w, w), F32),
            jax.ShapeDtypeStruct(probe.shape, F32),
        ),
        in_specs=[pl.BlockSpec(memory_space=smem)] + [whole] * 5,
        out_specs=(whole, whole),
        scratch_shapes=scratch,
        compiler_params=pltpu.CompilerParams(
            collective_id=0, has_side_effects=True, vmem_limit_bytes=48 * 2**20
        ),
    )(
        offsets.reshape(batches, 2),
        object_field.reshape(4, w, w),
        probe,
        kernel_phase,
        amplitudes.reshape(batches, w, w),
        jnp.asarray(dft_matrices(w)),
    )
    return obj.reshape(object_field.shape), new_probe


def solution(mesh):
    in_specs = (
        P(None, None, "row", "col"),
        P(),
        P(),
        P(None, "row", "col", None, None),
        P(None, "row", "col", None),
    )
    out_specs = (P(None, None, "row", "col"), P())
    return jax.shard_map(
        functools.partial(per_device, mesh.shape["row"], mesh.shape["col"]),
        mesh=mesh, in_specs=in_specs, out_specs=out_specs, check_vma=False,
    )
```

profile of v0, /device:TPU:0, one launch (start us, length us, event | category | flops | bytes accessed | tf_op | source)
XLA Modules:
  0.0 99.6 jit_solution(10217768345291274635)
XLA Ops:
  0.6 0.0 copy-start.5
  0.6 0.7 copy-done.5
  1.3 0.1 copy.8.off_ref
  1.4 0.0 copy-start
  1.4 1.0 %copy-done = f32[4,2,128,128]{3,2,1,0:T(8,128)S(1)} copy-done((f32[4,2,128,128]{3,2,1,0:T(8,128)S(1)}, f32[4,2,128,128]{3,2,1,0:T(8,128)}, u32[]{:S(2)}) %copy-start) | copy-done | bytes 524312
  2.4 0.0 copy-start.1
  2.4 1.0 %copy-done.1 = bf16[4,256,256]{2,1,0:T(8,128)(2,1)S(1)} copy-done((bf16[4,256,256]{2,1,0:T(8,128)(2,1)S(1)}, bf16[4,256,256]{2,1,0:T(8,128)(2,1)}, u32[]{:S(2)}) %copy-start.1) | copy-done | bytes 524312
  3.5 0.0 copy-start.2
  3.5 0.9 copy-done.2
  4.4 0.0 copy-start.3
  4.4 0.9 copy-done.3
  5.4 0.0 copy-start.4
  5.4 0.8 copy-done.4
  6.2 91.9 %shard_map.77 = (f32[4,128,128]{2,1,0:T(8,128)S(1)}, f32[4,2,128,128]{3,2,1,0:T(8,128)S(1)}) custom-call(s32[3,2]{1,0:T(4,128)S(1)} %copy.8.off_ref, f32[4,128,128]{2,1,0:T(8,128)S(1)} %bitcast.5, f32[4,2,128,128]{3,2,1,0:T(8,128)S(1)} %copy-done, f32[128,128]{1,0:T(8,128)S(1)} %copy-done.4, f32[3,128,128]{2,1,0:T(8,128)S(1)} %bitcast.6, ...), custom_call_target="tpu_custom_call" | custom-call | tf_op jit(solution)/shard_map/pallas_call | solution.py:435
  98.1 0.7 copy.11
  98.8 0.8 copy.12
Async XLA Ops:
  0.6 0.7 copy-start.5
  1.4 1.0 %copy-start = (f32[4,2,128,128]{3,2,1,0:T(8,128)S(1)}, f32[4,2,128,128]{3,2,1,0:T(8,128)}, u32[]{:S(2)}) copy-start(f32[4,2,128,128]{3,2,1,0:T(8,128)} %probe_ref.1) | copy-start | bytes 1572868
  2.4 1.0 %copy-start.1 = (bf16[4,256,256]{2,1,0:T(8,128)(2,1)S(1)}, bf16[4,256,256]{2,1,0:T(8,128)(2,1)}, u32[]{:S(2)}) copy-start(bf16[4,256,256]{2,1,0:T(8,128)(2,1)} %constant.2.clone.tab_ref) | copy-start | bytes 1572868
  3.5 0.9 copy-start.2
  4.4 0.9 copy-start.3
  5.4 0.8 copy-start.4
where the time goes:
time: 100 us; the launch traced here: 99.6 us
  Pallas kernels  91.9 us (92%)
  local copies, waits for them, and re-layouts  7.06 us (7%)
    pallas_call x1, Pallas kernels, per_device(): pl.pallas_call(functools.partial(kernel, n_row, n_col, batches, modes, st...  91.9 us
    unnamed x14, local copies, waits for them, and re-layouts  6.97 us

commit v1 on v0

--- a/solution.py
+++ b/solution.py
@@ -91,15 +91,29 @@
 
 def kernel(
     n_row, n_col, batches, modes, stages,
-    off_ref, obj_ref, probe_ref, phase_ref, amp_ref, tab_ref,
+    off_ref, obj_hbm, probe_hbm, phase_hbm, amp_hbm, tab_hbm,
     obj_out, probe_out,
     ext, ziel, grad, strip, from_row, from_col, from_corner,
-    phi_ref, kern_ref, pnow, acc, gat, *rest,
+    phi_ref, kern_ref, pnow, acc, gat, probe_ref, phase_ref, amp_ref, tab_ref, *rest,
 ):
     stage_bufs = rest[: len(stages)]
-    ex_send, ex_recv, rs_send, rs_recv, ag_send, ag_recv = rest[len(stages) :]
-    w = obj_ref.shape[-1]
+    in_sem, ex_send, ex_recv, rs_send, rs_recv, ag_send, ag_recv = rest[len(stages) :]
+    w = obj_out.shape[-1]
     full = w + 2 * OVL
+    loads = [
+        pltpu.make_async_copy(src, dst, in_sem.at[i])
+        for i, (src, dst) in enumerate(
+            (
+                (obj_hbm, grad.at[0, pl.ds(0, 4), pl.ds(OVL, w)]),
+                (phase_hbm, phase_ref),
+                (probe_hbm, probe_ref),
+                (tab_hbm, tab_ref),
+                (amp_hbm, amp_ref),
+            )
+        )
+    ]
+    for load in loads:
+        load.start()
     band = 2 * OVL
     row, col = lax.axis_index("row"), lax.axis_index("col")
 
@@ -157,58 +171,77 @@
     def swap(x):
         return pltpu.roll(x, w // 2, x.ndim - 1)
 
-    def send(e):
-        for p in range(2):
-            side, a, b = grad[e, 4 + p], grad[e, 2 * p], swap(grad[e, 2 * p + 1])
-            strip[e, 0, p] = jnp.where(left_part, side, jnp.where(low, a, b))
-            strip[e, 1, p] = jnp.where(left_part, jnp.where(high, a, b), side)
+    def rows_of(e, dr):
+        if e == 0:
+            return {-1: (OVL, OVL), 0: (OVL, w), 1: (w, OVL)}[dr]
+        if e == batches:
+            return {-1: (0, OVL), 0: (OVL, w), 1: (OVL + w, OVL)}[dr]
+        return {-1: (0, band), 0: (0, full), 1: (w, band)}[dr]
+
+    def parts_of(e, k, p):
+        dr, dc = SIDES[k]
+        first, count = rows_of(e, dr)
+        rows, to = pl.ds(first, count), pl.ds(0, count)
+        if dc == 0:
+            out = [(grad.at[e, pl.ds(2 * p, 2), rows], from_row.at[e, k, pl.ds(2 * p, 2), to], p)]
+            if 0 < e < batches:
+                out.append((grad.at[e, 4 + p, rows], from_row.at[e, k, 4 + p, to], 2 + p))
+            return out
+        side = 0 if dc < 0 else 1
+        if dr == 0:
+            return [(strip.at[e, side, p, rows], from_col.at[e, k - 2, p, to], p)]
+        return [(strip.at[e, side, p, rows], from_corner.at[e, k - 4, p, to], p)]
+
+    def copies_of(e, k, p):
+        dr, dc = SIDES[k]
+        return [
+            pltpu.make_async_remote_copy(
+                src_ref=src, dst_ref=dst,
+                send_sem=ex_send.at[e, k, i], recv_sem=ex_recv.at[e, k, i],
+                device_id=(row + dr, col + dc), device_id_type=MESH,
+            )
+            for src, dst, i in parts_of(e, k, p)
+        ]
+
+    def send(e, p):
+        side, a, b = grad[e, 4 + p], grad[e, 2 * p], swap(grad[e, 2 * p + 1])
+        strip[e, 0, p] = jnp.where(left_part, side, jnp.where(low, a, b))
+        strip[e, 1, p] = jnp.where(left_part, jnp.where(high, a, b), side)
         for k in range(8):
             dr, dc = SIDES[k]
 
             @pl.when(there(dr, dc))
             def _():
-                copy_of(e, k).start()
-
-    def copy_of(e, k):
-        dr, dc = SIDES[k]
-        rows = pl.ds(0 if dr < 0 else w, band)
-        if dc == 0:
-            src, dst = grad.at[e, :, rows], from_row.at[e, k]
-        elif dr == 0:
-            src, dst = strip.at[e, k - 2], from_col.at[e, k - 2]
-        else:
-            src, dst = strip.at[e, 0 if dc < 0 else 1, :, rows], from_corner.at[e, k - 4]
-        return pltpu.make_async_remote_copy(
-            src_ref=src, dst_ref=dst, send_sem=ex_send.at[e, k], recv_sem=ex_recv.at[e, k],
-            device_id=(row + dr, col + dc), device_id_type=MESH,
-        )
-
-    def receive(e, scale):
-        for f in range(6):
+                for c in copies_of(e, k, p):
+                    c.start()
+
+    def receive(e, scale, p):
+        for f in (2 * p, 2 * p + 1, 4 + p):
             ext[f] = ext[f] + scale * grad[e, f] if e else grad[e, f]
         for k in range(8):
             dr, dc = SIDES[k]
 
             @pl.when(there(-dr, -dc))
             def _():
-                copy_of(e, k).wait_recv()
-                rows = pl.ds(w if dr < 0 else 0, band)
+                for c in copies_of(e, k, p):
+                    c.wait_recv()
+                first, count = rows_of(e, dr)
+                rows = pl.ds(first - dr * w, count)
                 if dc == 0:
-                    for f in range(6):
-                        ext[f, rows] = ext[f, rows] + scale * from_row[e, k, f]
+                    for f in (2 * p, 2 * p + 1) + ((4 + p,) if 0 < e < batches else ()):
+                        ext[f, rows] = ext[f, rows] + scale * from_row[e, k, f, :count]
                     return
+                lp, lo, hi = left_part[:count], low[:count], high[:count]
                 if dr == 0:
-                    rows = pl.ds(0, full)
-                count = full if dr == 0 else band
-                lp, lo, hi = left_part[:count], low[:count], high[:count]
-                for p in range(2):
-                    x = from_col[e, k - 2, p] if dr == 0 else from_corner[e, k - 4, p]
-                    x = scale * x
-                    y = swap(x)
-                    edge, mine = (lo, lp) if dc > 0 else (hi, jnp.logical_not(lp))
-                    ext[4 + p, rows] = ext[4 + p, rows] + jnp.where(mine, x, 0.0)
-                    ext[2 * p, rows] = ext[2 * p, rows] + jnp.where(edge, x, 0.0)
-                    ext[2 * p + 1, rows] = ext[2 * p + 1, rows] + jnp.where(edge, y, 0.0)
+                    x = from_col[e, k - 2, p, :count]
+                else:
+                    x = from_corner[e, k - 4, p, :count]
+                x = scale * x
+                y = swap(x)
+                edge, mine = (lo, lp) if dc > 0 else (hi, jnp.logical_not(lp))
+                ext[4 + p, rows] = ext[4 + p, rows] + jnp.where(mine, x, 0.0)
+                ext[2 * p, rows] = ext[2 * p, rows] + jnp.where(edge, x, 0.0)
+                ext[2 * p + 1, rows] = ext[2 * p + 1, rows] + jnp.where(edge, y, 0.0)
 
     def sent(e):
         for k in range(8):
@@ -216,7 +249,9 @@
 
             @pl.when(there(dr, dc))
             def _():
-                copy_of(e, k).wait_send()
+                for p in range(2):
+                    for c in copies_of(e, k, p):
+                        c.wait_send()
 
     def base_of(s):
         rows = acc.shape[1]
@@ -278,33 +313,52 @@
         for c in ag_copies(q, s):
             c.wait()
 
-    def sum_steps(q):
+    def sum_steps():
         steps = []
         last = len(stages) - 1
         for s in range(last + 1):
-            steps.append((lambda s=s: rs_start(q, s), lambda s=s: rs_end(q, s)))
+            steps.append((lambda i, s=s: rs_start(i, s), lambda i, s=s: rs_end(i, s)))
         for s in range(last, -1, -1):
-            steps.append((lambda s=s: ag_start(q, s), lambda s=s: ag_end(q, s)))
+            steps.append((lambda i, s=s: ag_start(i, s), lambda i, s=s: ag_end(i, s)))
         return steps
 
     running = []
 
     def advance():
-        if running:
-            running.pop(0)[1]()
-            if running:
-                running[0][0]()
-
-    for f in range(6):
+        for part, steps in list(running):
+            steps.pop(0)[1](part)
+            if steps:
+                steps[0][0](part)
+            else:
+                running.remove((part, steps))
+
+    def begin(part):
+        steps = sum_steps()
+        steps[0][0](part)
+        running.append((part, steps))
+
+    for f in range(4):
+        grad[0, f, :OVL] = jnp.zeros((OVL, w), F32)
+        grad[0, f, OVL + w :] = jnp.zeros((OVL, w), F32)
+    for f in range(4, 6):
         grad[0, f] = jnp.zeros((full, w), F32)
-    for f in range(4):
-        grad[0, f, OVL : OVL + w] = obj_ref[f]
+    loads[0].wait()
     pl.semaphore_wait(barrier, expected)
-    send(0)
+    send(0, 0)
+    send(0, 1)
+    for load in loads[1:]:
+        load.wait()
     kern_ref[0] = jnp.cos(phase_ref[...])
     kern_ref[1] = jnp.sin(phase_ref[...])
     ziel[...] = jnp.zeros_like(ziel)
-    receive(0, 1.0)
+    receive(0, 1.0, 0)
+    receive(0, 1.0, 1)
+
+    half = modes // 2 if modes % 2 == 0 else modes
+    parts = modes // half
+
+    def sum_at(q, m, k):
+        return q * parts + m // half, (m % half * 2 + k) * w
 
     rate = PROBE_RATE / math.sqrt(n_row * n_col)
     kern = (kern_ref[0], kern_ref[1])
@@ -321,8 +375,8 @@
             previous = probe_ref if b == 2 else pnow
             for m in range(modes):
                 for k in range(2):
-                    at = (m * 2 + k) * w
-                    pnow[m, k] = previous[m, k] - rate * gat[b - 2, at : at + w]
+                    i, at = sum_at(b - 2, m, k)
+                    pnow[m, k] = previous[m, k] - rate * gat[i, at : at + w]
             source = pnow
         y0, x0 = off_ref[b, 0], off_ref[b, 1]
         start = x0 - OVL
@@ -354,41 +408,66 @@
         chi2 = dft([(v[0] * factor, v[1] * factor) for v in far], tables, True)
         advance()
         g2 = csum([conj_mul((phi_ref[m, 0], phi_ref[m, 1]), chi2[m]) for m in range(modes)])
-        spectrum = dft([conj_mul(o2, v) for v in chi2], tables, False)
-        chi1 = dft([cmul(v, conj_kern) for v in spectrum], tables, True)
-        advance()
-        probe = [(source[m, 0], source[m, 1]) for m in range(modes)]
-        g1 = csum([conj_mul(probe[m], chi1[m]) for m in range(modes)])
-        for f, g in enumerate((*g1, *g2)):
-            ziel[f, 2 * OVL : 2 * OVL + w] = g
         ahead = lax.rem(w + start, w)
         outside = (lane - start < 0) | (lane - start >= w)
-        others = []
-        for f in range(4):
-            moved = pltpu.roll(ziel[f, pl.ds(2 * OVL - y0, full), :], ahead, 1)
-            grad[b + 1, f] = jnp.where(row_ok & jnp.logical_not(outside), moved, 0.0)
-            others.append(jnp.where(outside, moved, 0.0))
-        for p in range(2):
-            grad[b + 1, 4 + p] = jnp.where(
-                side_ok, others[2 * p] + swap(others[2 * p + 1]), 0.0
-            )
-        send(b + 1)
+
+        def place(p, pair):
+            others = []
+            for f in (2 * p, 2 * p + 1):
+                ziel[f, 2 * OVL : 2 * OVL + w] = pair[f % 2]
+                moved = pltpu.roll(ziel[f, pl.ds(2 * OVL - y0, full), :], ahead, 1)
+                grad[b + 1, f] = jnp.where(row_ok & jnp.logical_not(outside), moved, 0.0)
+                others.append(jnp.where(outside, moved, 0.0))
+            grad[b + 1, 4 + p] = jnp.where(side_ok, others[0] + swap(others[1]), 0.0)
+            send(b + 1, p)
+
+        place(1, g2)
+        q = min(b, max(batches - 2, 0))
+        final = b == batches - 1
+        starts_sum = b != batches - 2 or batches == 1
+        g1 = None
+
+        def keep(group, chi1):
+            for m, v in zip(group, chi1):
+                g = conj_mul(o1, v)
+                for k in range(2):
+                    i, at = sum_at(q, m, k)
+                    place_at = pl.ds(at, w)
+                    acc[i, place_at] = g[k] if b == q else acc[i, place_at] + g[k]
+
+        kept = []
+        for part in range(parts):
+            group = range(part * half, part * half + half)
+            spectrum = dft([conj_mul(o2, chi2[m]) for m in group], tables, False)
+            chi1 = dft([cmul(v, conj_kern) for v in spectrum], tables, True)
+            if final:
+                keep(group, chi1)
+                if part:
+                    advance()
+                begin(q * parts + part)
+            else:
+                kept.append((group, chi1))
+            term = csum(
+                [conj_mul((source[m, 0], source[m, 1]), v) for m, v in zip(group, chi1)]
+            )
+            g1 = term if g1 is None else csum([g1, term])
+        if not final:
+            advance()
+        place(0, g1)
         advance()
-        q = min(b, max(batches - 2, 0))
-        for m in range(modes):
-            g = conj_mul(o1, chi1[m])
-            for k in range(2):
-                at = pl.ds((m * 2 + k) * w, w)
-                acc[q, at] = g[k] if b == q else acc[q, at] + g[k]
-        if b != batches - 2 or batches == 1:
+        for group, chi1 in kept:
+            keep(group, chi1)
+        if starts_sum and not final:
             while running:
                 advance()
-            running.extend(sum_steps(q))
-            running[0][0]()
-        receive(b + 1, -OBJECT_RATE)
-        if b < batches - 1:
+            for part in range(parts):
+                begin(q * parts + part)
+        receive(b + 1, -OBJECT_RATE, 1)
+        if final:
             advance()
-        if b == batches - 1:
+        receive(b + 1, -OBJECT_RATE, 0)
+        advance()
+        if final:
             for f in range(4):
                 obj_out[f] = ext[f, OVL : OVL + w]
 
@@ -398,8 +477,8 @@
     last = pnow if batches > 2 else probe_ref
     for m in range(modes):
         for k in range(2):
-            at = (m * 2 + k) * w
-            probe_out[m, k] = last[m, k] - rate * gat[q, at : at + w]
+            i, at = sum_at(q, m, k)
+            probe_out[m, k] = last[m, k] - rate * gat[i, at : at + w]
     for e in range(batches + 1):
         sent(e)
 
@@ -408,9 +487,10 @@
     batches = amplitudes.shape[0]
     modes, _, w, _ = probe.shape
     full = w + 2 * OVL
-    rows = modes * 2 * w
+    parts = 2 if modes % 2 == 0 else 1
+    rows = modes * 2 * w // parts
     stages = stages_of(rows, n_row, n_col)
-    sums = max(batches - 1, 1)
+    sums = max(batches - 1, 1) * parts
     most = max(n for _, n, _, _ in stages)
     vmem, smem = pltpu.VMEM, pltpu.SMEM
     dma = pltpu.SemaphoreType.DMA
@@ -427,10 +507,14 @@
         vmem((modes, 2, w, w), F32),
         vmem((sums, rows, w), F32),
         vmem((sums, rows, w), F32),
+        vmem(probe.shape, F32),
+        vmem((w, w), F32),
+        vmem((batches, w, w), F32),
+        vmem((4, 2 * w, 2 * w), BF16),
     ]
     for _, n, scatter, after in stages:
         scratch.append(vmem((sums, n - 1 if scatter else n, after, w), F32))
-    scratch += [dma((batches + 1, 8))] * 2 + [dma((sums, len(stages), most))] * 4
+    scratch += [dma((5,))] + [dma((batches + 1, 8, 4))] * 2 + [dma((sums, len(stages), most))] * 4
     whole = pl.BlockSpec(memory_space=vmem)
     obj, new_probe = pl.pallas_call(
         functools.partial(kernel, n_row, n_col, batches, modes, stages),
@@ -438,7 +522,7 @@
             jax.ShapeDtypeStruct((4, w, w), F32),
             jax.ShapeDtypeStruct(probe.shape, F32),
         ),
-        in_specs=[pl.BlockSpec(memory_space=smem)] + [whole] * 5,
+        in_specs=[pl.BlockSpec(memory_space=smem)] + [pl.BlockSpec(memory_space=pltpu.HBM)] * 5,
         out_specs=(whole, whole),
         scratch_shapes=scratch,
         compiler_params=pltpu.CompilerParams(

time: 100 us -> 90.6 us (0.906)
  Pallas kernels: 91.9 us -> 82.5 us
    pallas_call x1, Pallas kernels: 91.9 us -> 82.5 us  [per_device(): pl.pallas_call(functools.partial(kernel, n_row, n_col, batches, modes, st...]
where the time goes in v1:
time: 90.6 us; the launch traced here: 90.2 us
  Pallas kernels  82.5 us (91%)
  local copies, waits for them, and re-layouts  7.06 us (8%)
    pallas_call x1, Pallas kernels, per_device(): pl.pallas_call(functools.partial(kernel, n_row, n_col, batches, modes, st...  82.5 us
    unnamed x14, local copies, waits for them, and re-layouts  6.97 us

profile of v1, /device:TPU:0, one launch (start us, length us, event | category | flops | bytes accessed | tf_op | source)
XLA Modules:
  0.0 90.2 jit_solution(2675883587831093959)
XLA Ops:
  0.6 0.0 copy-start.5
  0.6 0.7 copy-done.5
  1.3 0.1 copy.8.off_ref
  1.4 0.0 copy-start
  1.4 1.0 %copy-done = f32[4,2,128,128]{3,2,1,0:T(8,128)S(1)} copy-done((f32[4,2,128,128]{3,2,1,0:T(8,128)S(1)}, f32[4,2,128,128]{3,2,1,0:T(8,128)}, u32[]{:S(2)}) %copy-start) | copy-done | bytes 524312
  2.4 0.0 copy-start.1
  2.4 1.0 %copy-done.1 = bf16[4,256,256]{2,1,0:T(8,128)(2,1)S(1)} copy-done((bf16[4,256,256]{2,1,0:T(8,128)(2,1)S(1)}, bf16[4,256,256]{2,1,0:T(8,128)(2,1)}, u32[]{:S(2)}) %copy-start.1) | copy-done | bytes 524312
  3.5 0.0 copy-start.2
  3.5 0.9 %copy-done.2 = f32[2,2,128,128]{3,2,1,0:T(8,128)S(1)} copy-done((f32[2,2,128,128]{3,2,1,0:T(8,128)S(1)}, f32[2,2,128,128]{3,2,1,0:T(8,128)}, u32[]{:S(2)}) %copy-start.2) | copy-done | bytes 262168
  4.4 0.0 copy-start.3
  4.4 0.9 %copy-done.3 = f32[3,1,1,128,128]{4,3,2,1,0:T(8,128)S(1)} copy-done((f32[3,1,1,128,128]{4,3,2,1,0:T(8,128)S(1)}, f32[3,1,1,128,128]{4,3,2,1,0:T(8,128)}, u32[]{:S(2)}) %copy-start.3) | copy-done | bytes 196632
  5.4 0.0 copy-start.4
  5.4 0.8 copy-done.4
  6.2 82.5 %shard_map.77 = (f32[4,128,128]{2,1,0:T(8,128)S(1)}, f32[4,2,128,128]{3,2,1,0:T(8,128)S(1)}) custom-call(s32[3,2]{1,0:T(4,128)S(1)} %copy.8.off_ref, f32[4,128,128]{2,1,0:T(8,128)S(1)} %bitcast.5, f32[4,2,128,128]{3,2,1,0:T(8,128)S(1)} %copy-done, f32[128,128]{1,0:T(8,128)S(1)} %copy-done.4, f32[3,128,128]{2,1,0:T(8,128)S(1)} %bitcast.6, ...), custom_call_target="tpu_custom_call" | custom-call | tf_op jit(solution)/shard_map/pallas_call | solution.py:519
  88.7 0.7 copy.11
  89.5 0.8 copy.12
Async XLA Ops:
  0.6 0.7 copy-start.5
  1.4 1.0 %copy-start = (f32[4,2,128,128]{3,2,1,0:T(8,128)S(1)}, f32[4,2,128,128]{3,2,1,0:T(8,128)}, u32[]{:S(2)}) copy-start(f32[4,2,128,128]{3,2,1,0:T(8,128)} %probe_hbm.1) | copy-start | bytes 1572868
  2.4 1.0 %copy-start.1 = (bf16[4,256,256]{2,1,0:T(8,128)(2,1)S(1)}, bf16[4,256,256]{2,1,0:T(8,128)(2,1)}, u32[]{:S(2)}) copy-start(bf16[4,256,256]{2,1,0:T(8,128)(2,1)} %constant.2.clone.tab_hbm) | copy-start | bytes 1572868
  3.5 0.9 %copy-start.2 = (f32[2,2,128,128]{3,2,1,0:T(8,128)S(1)}, f32[2,2,128,128]{3,2,1,0:T(8,128)}, u32[]{:S(2)}) copy-start(f32[2,2,128,128]{3,2,1,0:T(8,128)} %param.6) | copy-start | bytes 786436
  4.4 0.9 %copy-start.3 = (f32[3,1,1,128,128]{4,3,2,1,0:T(8,128)S(1)}, f32[3,1,1,128,128]{4,3,2,1,0:T(8,128)}, u32[]{:S(2)}) copy-start(f32[3,1,1,128,128]{4,3,2,1,0:T(8,128)} %param.9) | copy-start | bytes 589828
  5.4 0.8 copy-start.4

commit v2 on v1

--- a/solution.py
+++ b/solution.py
@@ -526,7 +526,7 @@
         out_specs=(whole, whole),
         scratch_shapes=scratch,
         compiler_params=pltpu.CompilerParams(
-            collective_id=0, has_side_effects=True, vmem_limit_bytes=48 * 2**20
+            collective_id=0, has_side_effects=True, vmem_limit_bytes=64 * 2**20 - 64 * 2**10
         ),
     )(
         offsets.reshape(batches, 2),

time: 90.6 us -> 87.8 us (0.969)
  local copies, waits for them, and re-layouts: 7.06 us -> 3.86 us
    unnamed x14 -> x6, local copies, waits for them, and re-layouts: 6.97 us -> 3.2 us
where the time goes in v2:
time: 87.8 us; the launch traced here: 87.6 us
  Pallas kernels  83.1 us (95%)
  local copies, waits for them, and re-layouts  3.86 us (4%)
    pallas_call x1, Pallas kernels, per_device(): pl.pallas_call(functools.partial(kernel, n_row, n_col, batches, modes, st...  83.1 us
    unnamed x6, local copies, waits for them, and re-layouts  3.2 us

profile of v2, /device:TPU:0, one launch (start us, length us, event | category | flops | bytes accessed | tf_op | source)
XLA Modules:
  0.0 87.6 jit_solution(5016313169697618361)
XLA Ops:
  0.6 0.0 copy-start.1
  0.6 0.7 copy-done.1
  1.3 0.7 copy.8.off_ref
  2.0 83.1 %shard_map.77 = (f32[4,128,128]{2,1,0:T(8,128)}, f32[4,2,128,128]{3,2,1,0:T(8,128)}) custom-call(s32[3,2]{1,0:T(4,128)} %copy.8.off_ref, f32[4,128,128]{2,1,0:T(8,128)} %bitcast.5, f32[4,2,128,128]{3,2,1,0:T(8,128)} %probe_hbm.1, f32[128,128]{1,0:T(8,128)} %phase_hbm.1, f32[3,128,128]{2,1,0:T(8,128)} %bitcast.6, bf16[4,256,256]{2,1,0:T(8,128)(2,1)} %constant.2.clone.tab_hbm), custom_call_target="tpu_custom_call" | custom-call | tf_op jit(solution)/shard_map/pallas_call | solution.py:519
  85.1 0.0 copy-start
  85.1 1.7 %copy.11 = f32[2,2,128,128]{3,2,1,0:T(8,128)} copy(f32[2,2,128,128]{3,2,1,0:T(8,128)} %bitcast.4) | data formatting | bytes 524288
  86.8 0.0 copy-done
  86.8 0.8 copy.12
Async XLA Ops:
  0.6 0.7 copy-start.1
  85.1 1.7 %copy-start = (f32[4,2,128,128]{3,2,1,0:T(8,128)S(1)}, f32[4,2,128,128]{3,2,1,0:T(8,128)}, u32[]{:S(2)}) copy-start(f32[4,2,128,128]{3,2,1,0:T(8,128)} %get-tuple-element.9) | copy-start | bytes 1572868

commit v3 on v2

--- a/solution.py
+++ b/solution.py
@@ -354,7 +354,7 @@
     receive(0, 1.0, 0)
     receive(0, 1.0, 1)
 
-    half = modes // 2 if modes % 2 == 0 else modes
+    half = 1
     parts = modes // half
 
     def sum_at(q, m, k):
@@ -436,15 +436,17 @@
                     acc[i, place_at] = g[k] if b == q else acc[i, place_at] + g[k]
 
         kept = []
-        for part in range(parts):
-            group = range(part * half, part * half + half)
+        step = 2 if final and modes % 2 == 0 else modes
+        for first in range(0, modes, step):
+            group = range(first, first + step)
             spectrum = dft([conj_mul(o2, chi2[m]) for m in group], tables, False)
             chi1 = dft([cmul(v, conj_kern) for v in spectrum], tables, True)
             if final:
                 keep(group, chi1)
-                if part:
+                if first:
                     advance()
-                begin(q * parts + part)
+                for part in range(first // half, (first + step) // half):
+                    begin(q * parts + part)
             else:
                 kept.append((group, chi1))
             term = csum(
@@ -487,7 +489,7 @@
     batches = amplitudes.shape[0]
     modes, _, w, _ = probe.shape
     full = w + 2 * OVL
-    parts = 2 if modes % 2 == 0 else 1
+    parts = modes
     rows = modes * 2 * w // parts
     stages = stages_of(rows, n_row, n_col)
     sums = max(batches - 1, 1) * parts

time: 87.8 us -> 91.6 us (1.043)
  Pallas kernels: 83.1 us -> 86.9 us
    pallas_call x1, Pallas kernels: 83.1 us -> 86.9 us  [per_device(): pl.pallas_call(functools.partial(kernel, n_row, n_col, batches, modes, st...]
where the time goes in v3:
time: 91.6 us; the launch traced here: 91.4 us
  Pallas kernels  86.9 us (95%)
  local copies, waits for them, and re-layouts  3.86 us (4%)
    pallas_call x1, Pallas kernels, per_device(): pl.pallas_call(functools.partial(kernel, n_row, n_col, batches, modes, st...  86.9 us
    unnamed x6, local copies, waits for them, and re-layouts  3.2 us

profile of v3, /device:TPU:0, one launch (start us, length us, event | category | flops | bytes accessed | tf_op | source)
XLA Modules:
  0.0 91.4 jit_solution(7521002839704208887)
XLA Ops:
  0.6 0.0 copy-start.1
  0.6 0.7 copy-done.1
  1.3 0.7 copy.8.off_ref
  2.0 86.9 %shard_map.77 = (f32[4,128,128]{2,1,0:T(8,128)}, f32[4,2,128,128]{3,2,1,0:T(8,128)}) custom-call(s32[3,2]{1,0:T(4,128)} %copy.8.off_ref, f32[4,128,128]{2,1,0:T(8,128)} %bitcast.5, f32[4,2,128,128]{3,2,1,0:T(8,128)} %probe_hbm.1, f32[128,128]{1,0:T(8,128)} %phase_hbm.1, f32[3,128,128]{2,1,0:T(8,128)} %bitcast.6, bf16[4,256,256]{2,1,0:T(8,128)(2,1)} %constant.2.clone.tab_hbm), custom_call_target="tpu_custom_call" | custom-call | tf_op jit(solution)/shard_map/pallas_call | solution.py:521
  88.9 0.0 copy-start
  88.9 1.7 %copy.11 = f32[2,2,128,128]{3,2,1,0:T(8,128)} copy(f32[2,2,128,128]{3,2,1,0:T(8,128)} %bitcast.4) | data formatting | bytes 524288
  90.6 0.0 copy-done
  90.6 0.8 copy.12
Async XLA Ops:
  0.6 0.7 copy-start.1
  88.9 1.7 %copy-start = (f32[4,2,128,128]{3,2,1,0:T(8,128)S(1)}, f32[4,2,128,128]{3,2,1,0:T(8,128)}, u32[]{:S(2)}) copy-start(f32[4,2,128,128]{3,2,1,0:T(8,128)} %get-tuple-element.9) | copy-start | bytes 1572868
